TPU v7x, 256 devices: a whole 4x4x8 slice. The times are simulated.
256 devices in a mesh: tile: 64 (over y, z_hi, x), mem: 4 (over z_lo, core).
Axes of the slice: x: 4, y: 4, z: 8 (z_hi: 4, z_lo: 2; z = z_hi * 2 + z_lo), core: 2. Of those that a mesh axis runs over, the one named last changes fastest.
Arguments:
- perturbations: bfloat16 [32, 16, 512, 256], P('mem', None, 'tile'), may hold values from -6 to 6
- classes: int32 [512, 256], P('tile'), may hold values from 0 to 3
- obs_tile: int32 [65536, 1], P('tile'), may hold values from 0 to 63; in each aligned block of 1024 rows (0 to 1023, 1024 to 2047, ...) at most 48 rows name the same one
- obs_cells: int32 [4, 65536], P(None, 'tile'), may hold values from 0 to 2047
- obs_interp: float32 [4, 65536], P(None, 'tile'), may hold values from 0.1 to 0.6
- obs_jacobian: float32 [16, 65536], P(None, 'tile'), may hold values from 0.1 to 1
- innovation: float32 [65536], P('tile'), may hold values from -10 to 10
- inv_error: float32 [65536], P('tile'), may hold values from 0.5 to 4
Outputs:
- control: float32 [32, 16, 512, 256], P('mem', None, 'tile')
- increment: float32 [16, 512, 256], P('mem', 'tile')
Inputs may be any that keep to these rules, and one draw needn't show every extreme that they name: `obs_tile`: each device's 1024 rows name at most 48 observations in one band; some band gets exactly 48 from some device.
All inputs are finite; a program needn't handle non-finite values.
Results may differ from a plain program's by a relative error of at most 0.0003.
Values sent between devices are 32-bit elements; how exact they have to be, the bound alone decides.
A program may use at most 64 MiB of HBM per device.

v0:
```python
import functools
import math

import jax
import jax.numpy as jnp
from jax import lax
from jax.experimental import pallas as pl
from jax.experimental.pallas import tpu as pltpu
from jax.sharding import PartitionSpec as P

MESH = pl.DeviceIdType.MESH
BF = jnp.bfloat16
F32 = jnp.float32
DIFFUSIVITIES = (0.06, 0.1, 0.15, 0.22)
STEP = 0.5
MOST = 48
FEATURES = 32
HALO = 4
LANES = 128

(A2A, KAP_U, KAP_D, OBS, AC0, AZ0, AU0, AD0, FZ0, FU0, FD0, CR0, RZ0, RU0, RD0, YS,
 AC1, AZ1, AU1, AD1, FZ1, FU1, FD1, CR1, RZ1, RU1, RD1, PERT) = range(28)
PARTS = ((0, 32), (32, 64), (64, 128))
EARLY = 1
N_SEM = PERT + 8 * len(PARTS)


def nt(a, b):
    return lax.dot_general(a, b, (((1,), (1,)), ((), ())), preferred_element_type=F32)


def nn(a, b):
    return jnp.dot(a, b, preferred_element_type=F32)


def split2(x):
    hi = x.astype(BF).astype(F32)
    return hi, x - hi


def kernel(
    tiles, groups, members,
    pert_hbm, classes_hbm, target_hbm, cells_hbm, interp_hbm, jac_hbm, innov_hbm, inv_hbm,
    control_ref, incr_ref,
    pert_ref, classes_ref, target_ref, cells_ref, interp_ref, jac_ref, innov_ref, inv_ref,
    perm, pay, val, out_buf, in_buf, feat, onehot, acols, acc,
    pert, stage, kap_rows, kap, ikap,
    x0, x1, up, vp, cr0, cs0, rz0, ru0, rd0, cr1, cs1, rz1, ru1, rd1, y_own, y_far, flat, ready, relay,
    ssem, rsem, lsem,
):
    t = lax.axis_index("tile")
    j = lax.axis_index("mem")
    north, south = lax.rem(t + tiles - 1, tiles), lax.rem(t + 1, tiles)
    cores = 2
    chip, core = j // cores, lax.rem(j, cores)
    slots = MOST // cores
    levels = 16
    scale = 1.0 / math.sqrt(members * groups - 1)
    obs = pay.shape[1]
    early = EARLY

    sibling = j + 1 - 2 * core
    across = lax.rem(j + cores, groups)

    def peer(d):
        return lax.rem(j + d, groups)

    def band(d):
        return lax.rem(t + d, tiles)

    def send(src, dst, k, tile, mem, k_out=None):
        pltpu.make_async_remote_copy(
            src_ref=src, dst_ref=dst, send_sem=ssem.at[k if k_out is None else k_out], recv_sem=rsem.at[k],
            device_id={"tile": tile, "mem": mem}, device_id_type=MESH,
        ).start()

    def arrived(like, k):
        pltpu.make_async_copy(like, like, rsem.at[k]).wait()

    def sent(like, k):
        pltpu.make_async_copy(like, like, ssem.at[k]).wait()

    fetches = [
        pltpu.make_async_copy(source, into, lsem.at[1 + k])
        for k, (source, into) in enumerate((
            (target_hbm, target_ref), (cells_hbm, cells_ref), (interp_hbm, interp_ref),
            (jac_hbm, jac_ref), (innov_hbm, innov_ref), (inv_hbm, inv_ref),
            (pert_hbm, pert_ref), (classes_hbm, classes_ref),
        ))
    ]
    for fetch in fetches:
        fetch.start()

    barrier = pltpu.get_barrier_semaphore()

    def greet(tile, mem):
        pl.semaphore_signal(
            barrier, inc=1, device_id={"tile": tile, "mem": mem}, device_id_type=MESH
        )

    def greet_band(d, carry):
        greet(band(d), j)
        return carry

    lax.fori_loop(1, tiles, greet_band, 0, unroll=9)
    for d in range(1, groups):
        greet(t, peer(d))
    greet(north, across)
    greet(south, across)

    row_id = lax.broadcasted_iota(jnp.int32, (256, 256), 0)
    col_id = lax.broadcasted_iota(jnp.int32, (256, 256), 1)
    perm[0] = jnp.where(col_id == (row_id & 1) * 128 + (row_id >> 1), 1.0, 0.0).astype(BF)
    perm[1] = jnp.where(row_id == (col_id & 1) * 128 + (col_id >> 1), 1.0, 0.0).astype(BF)

    for fetch in fetches[:6]:
        fetch.wait()

    target = target_ref[...]
    bands = lax.broadcasted_iota(jnp.int32, (tiles, obs), 0)
    member_of = jnp.where(target == bands, 1.0, 0.0)
    member_bf = member_of.astype(BF)
    before = jnp.where(row_id < col_id, 1.0, 0.0).astype(BF)
    base = jnp.zeros((tiles, 1), F32)
    ranks = []
    for b in range(obs // 256):
        part = slice(b * 256, (b + 1) * 256)
        count = nn(member_bf[:, part], before) + base
        ranks.append(jnp.sum(member_of[:, part] * count, axis=0, keepdims=True))
        base = base + jnp.sum(member_of[:, part], axis=1, keepdims=True)
    rank = jnp.concatenate(ranks, axis=1).astype(jnp.int32) - core * slots

    pay[0:16, :] = jac_ref[...]
    pay[16:24, :] = jnp.concatenate([cells_ref[...].astype(F32), interp_ref[...]], axis=0)
    pay[24:32, :] = jnp.concatenate(
        [innov_ref[...], inv_ref[...], jnp.zeros((6, obs), F32)], axis=0
    )
    whole = pay[...]
    high = whole.astype(BF).astype(F32)
    rest = whole - high
    middle = rest.astype(BF).astype(F32)
    low = rest - middle
    for q in range(slots):
        mine = rank == q
        for k, piece in enumerate((high, middle, low)):
            val[k, q * FEATURES : (q + 1) * FEATURES, :] = jnp.where(mine, piece, 0.0).astype(BF)
    packed = nt(member_bf, val[0]) + nt(member_bf, val[1]) + nt(member_bf, val[2])
    out_buf[:, 0, :] = packed

    for fetch in fetches[6:]:
        fetch.wait()

    def arrange(m, carry):
        block = pert_ref[m].astype(F32).reshape(levels * 8, 256).astype(BF)
        moved = nn(block, perm[0])
        stage[0] = moved[:, :LANES]
        stage[1] = moved[:, LANES:]
        for r in range(8):
            for lh in range(2):
                at = pl.ds(pl.multiple_of(m * levels + lh * 8, 8), 8)
                for h in range(2):
                    pert[HALO + r, h, at, :] = stage[h, pl.ds(lh * 64 + r, 8, stride=8), :]
        return carry

    lax.fori_loop(0, members, arrange, 0)

    classes = nn(classes_ref[...].astype(F32).astype(BF), perm[0])
    kappa = jnp.zeros(classes.shape, F32)
    for position, coefficient in enumerate(DIFFUSIVITIES):
        kappa = kappa + jnp.where(classes == float(position), coefficient, 0.0)
    kap_rows[1] = kappa

    pl.semaphore_wait(barrier, tiles - 1 + groups - 1 + 2)

    along_x = lax.rem(t, 4)
    ways = (
        (8, 0, south, 3, -3, 4),
        (4, 12, north, 0, 3, -4),
    )

    def edge(first_row, lo, hi):
        return pert.at[pl.ds(first_row, 4), :, pl.ds(lo, hi - lo)]

    def shares(part):
        lo, hi = PARTS[part]
        middle = (lo + hi) // 2
        return (lo, middle), (middle, hi)

    def key_of(way, part):
        return PERT + (way * len(PARTS) + part) * 4

    def waiting(way, part):
        lo, hi = shares(part)[1]
        return relay.at[way, :, :, pl.ds(PARTS[part][0] // 2, hi - lo)]

    def send_part(part):
        one, two = shares(part)
        for way, (here, there, to, wraps, hop, onward) in enumerate(ways):
            key = key_of(way, part)

            @pl.when(along_x == wraps)
            def _():
                send(edge(here, *two), waiting(way, part), key + 2, band(hop + tiles), j)

            send(edge(here, *one), edge(there, *one), key, to, j)

            @pl.when(along_x != wraps)
            def _():
                send(edge(here, *two), edge(there, *two), key + 1, to, j)

    def forward_part(part):
        two = shares(part)[1]
        for way, (here, there, to, wraps, hop, onward) in enumerate(ways):
            key = key_of(way, part)

            @pl.when(along_x == 3 - wraps)
            def _():
                arrived(waiting(way, part), key + 2)
                send(
                    waiting(way, part), edge(there, *two), key + 1, band(onward + tiles), j, key + 3
                )

    def part_arrived(part):
        one, two = shares(part)
        for way, (here, there, to, wraps, hop, onward) in enumerate(ways):
            arrived(edge(there, *one), key_of(way, part))
            arrived(edge(there, *two), key_of(way, part) + 1)

    def part_sent(part):
        one, two = shares(part)
        for way, (here, there, to, wraps, hop, onward) in enumerate(ways):
            key = key_of(way, part)
            sent(edge(here, *one), key)

            @pl.when(along_x == wraps)
            def _():
                sent(edge(here, *two), key + 2)

            @pl.when(along_x != wraps)
            def _():
                sent(edge(here, *two), key + 1)

            @pl.when(along_x == 3 - wraps)
            def _():
                sent(waiting(way, part), key + 3)

    send(kap_rows.at[1], kap_rows.at[0], KAP_U, south, j)
    send(kap_rows.at[1], kap_rows.at[2], KAP_D, north, j)
    for part in range(early):
        send_part(part)

    def send_band(d, carry):
        send(out_buf.at[band(d)], in_buf.at[core, t], A2A, band(d), j)
        return carry

    lax.fori_loop(1, tiles, send_band, 0, unroll=9)
    for part in range(early, len(PARTS)):
        send_part(part)
    for part in range(early):
        forward_part(part)
    own = pltpu.make_async_copy(out_buf.at[t], in_buf.at[core, t], lsem.at[0])
    own.start()
    arrived(kap_rows.at[0], KAP_U)
    arrived(kap_rows.at[2], KAP_D)
    for r in range(16):
        block, row = divmod(r + 4, 8)
        line = kap_rows[block, row : row + 1, :]
        if r < 4:
            line = jnp.where(t == 0, 0.0, line)
        if r >= 12:
            line = jnp.where(t == tiles - 1, 0.0, line)
        for h in range(2):
            wide = jnp.broadcast_to(line[:, h * LANES : (h + 1) * LANES], (8, LANES))
            kap[r, h] = wide
            if 4 <= r < 12:
                ikap[r - 4, h] = 1.0 / wide

    own.wait()
    arrived(in_buf.at[core, pl.ds(0, tiles - 1)], A2A)
    send(in_buf.at[core], in_buf.at[core], OBS, t, sibling)
    for part in range(early, len(PARTS)):
        forward_part(part)

    blocks = MOST * tiles // LANES
    per_core = blocks // cores

    def unpack(source):
        for g in range(0, slots * FEATURES // LANES, 2):
            both = jnp.concatenate(
                [in_buf[source, :, 0, n * LANES : (n + 1) * LANES] for n in (g, g + 1)], axis=0
            ).T
            for b in range(LANES // FEATURES):
                at = source * per_core + g * 2 + b
                feat[at] = both[b * FEATURES : (b + 1) * FEATURES, :]

    along = 4

    def in_turn(step, start=0, count=blocks):
        def several(i, carry):
            step([start + i * along + n for n in range(along)])
            return carry

        lax.fori_loop(0, count // along, several, 0)

    my_levels = pl.ds(pl.multiple_of(chip * 8, 8), 8)

    def hits(b, c):
        cell = feat[b, 16 + c : 17 + c, :].astype(jnp.int32)
        row = jnp.where((cell & 1) == core, cell >> 8, -1)
        rows = lax.broadcasted_iota(jnp.int32, (8, 8, LANES), 0)
        return rows == row.reshape(1, 1, LANES)

    def build(which):
        for b in which:
            for c in range(4):
                low = (feat[b, 16 + c : 17 + c, :].astype(jnp.int32) & 255) >> 1
                spot = lax.broadcasted_iota(jnp.int32, (LANES, LANES), 0) == low
                onehot[b, :, c * LANES : (c + 1) * LANES] = jnp.where(spot, 1.0, 0.0).astype(BF)

    def adjoint_obs(which, residual):
        for n, b in enumerate(which):
            z = residual(b)
            jac = feat[b, my_levels, :]
            for c in range(4):
                value = jac * (feat[b, 20 + c : 21 + c, :] * z)
                mask = hits(b, c)
                for k, piece in enumerate(split2(value)):
                    wide = jnp.where(mask, piece.reshape(1, 8, LANES), 0.0).reshape(64, LANES)
                    acols[n, k * 64 : (k + 1) * 64, c * LANES : (c + 1) * LANES] = wide.astype(BF)
        total = acc[...]
        for n, b in enumerate(which):
            total = total + nt(acols[n], onehot[b])
        acc[...] = total

    def summed():
        both = acc[...]
        return (both[:64] + both[64:]).reshape(8, 8, LANES)

    def first(which):
        build(which)
        adjoint_obs(which, lambda b: -(feat[b, 25:26, :] * feat[b, 24:25, :]))

    acc[...] = jnp.zeros(acc.shape, F32)
    unpack(core)
    in_turn(first, core * per_core, per_core)
    arrived(in_buf.at[1 - core], OBS)
    unpack(1 - core)
    in_turn(first, (1 - core) * per_core, per_core)
    x0[j, pl.ds(HALO, 8)] = summed()

    def spread(x, s_core, s_across, s_up, s_down, f_across, f_up, f_down):
        here = x.at[j, pl.ds(HALO, 8)]
        for to in (j, across):
            send(x.at[j, pl.ds(8, 4)], x.at[j, pl.ds(0, 4)], s_up, south, to)
            send(x.at[j, pl.ds(4, 4)], x.at[j, pl.ds(12, 4)], s_down, north, to)
        send(here, here, s_across, t, across)
        send(here, here, s_core, t, sibling)
        got = x.at[across, pl.ds(HALO, 8)]
        arrived(got, s_across)
        send(got, got, f_across, t, sibling)
        for key, forward, first_row in ((s_up, f_up, 0), (s_down, f_down, 12)):
            rows = pl.ds(first_row, 4)
            arrived(x.at[pl.ds(0, 2), rows], key)
            for half in range(2):
                edge = x.at[half * cores + core, rows]
                send(edge, edge, forward, t, sibling)
        arrived(here, s_core)
        arrived(got, f_across)
        arrived(x.at[pl.ds(0, 2), pl.ds(0, 4)], f_up)
        arrived(x.at[pl.ds(0, 2), pl.ds(12, 4)], f_down)

    spread(x0, AC0, AZ0, AU0, AD0, FZ0, FU0, FD0)
    for part in range(len(PARTS) - 1):
        part_arrived(part)

    def sweep(f, lo, hi):
        out = {}
        for r in range(lo, hi):
            here = f.get(r)
            beside = [f[n] for n in (r - 1, r + 1) if n in f]
            pair = []
            for h in range(2):
                terms = [row[h] for row in beside]
                if here is not None:
                    other = here[1 - h]
                    terms.append(other + pltpu.roll(other, (1, LANES - 1)[h], 1))
                beside_all = functools.reduce(jnp.add, terms)
                if here is None:
                    pair.append(kap[r, h] * beside_all)
                else:
                    pair.append(here[h] + kap[r, h] * (beside_all - 4.0 * here[h]))
            out[r] = pair
        return out

    def local_pass(x, control_out):
        up[...] = jnp.zeros(up.shape, F32)
        together = 4
        turns = 2 * members // together

        def group(i, carry):
            ids = []
            for g in range(together):
                lh, m = g % 2, i * (together // 2) + g // 2
                ids.append((lh, m, pl.ds(pl.multiple_of(m * levels + lh * 8, 8), 8)))
            fields = [
                {
                    r: [kap[r, h] * pert[r, h, at, :] * x[lh * 2 + h, r] for h in range(2)]
                    for r in range(16)
                }
                for lh, m, at in ids
            ]
            for k in range(4):
                fields = [sweep(f, k + 1, 15 - k) for f in fields]
            fields = [
                {r: [f[r][h] * ikap[r - HALO, h] for h in range(2)] for r in f} for f in fields
            ]
            if control_out:
                for f, (lh, m, at) in zip(fields, ids):
                    for r in range(8):
                        place_at = pl.ds(m * 128 + lh * 64 + r, 8, stride=8)
                        for h in range(2):
                            flat[h, place_at, :] = f[HALO + r][h]
            for k in range(4):
                fields = [sweep(f, 3 - k, 13 + k) for f in fields]
            for r in range(16):
                for h in range(2):
                    for half in range(2):
                        terms = [
                            pert[r, h, at, :] * f[r][h]
                            for f, (lh, m, at) in zip(fields, ids)
                            if lh == half
                        ]
                        up[half * 2 + h, r] += functools.reduce(jnp.add, terms)
            return carry

        lax.fori_loop(0, turns // 2, group, 0)
        if not control_out:
            part_arrived(len(PARTS) - 1)
        lax.fori_loop(turns // 2, turns, group, 0)

    def reduce_in_chip(source, from_core, key):
        for half in range(2):
            send(source.at[half * cores + 1 - core], from_core.at[half], key, t, sibling)

    def reduce_out(source, from_core, chip_sum, from_chip, from_north, from_south, keys):
        key, k_across, k_up, k_down = keys
        arrived(from_core, key)
        for half in range(2):
            chip_sum[half] = source[half * cores + core] + from_core[half]
        for half in range(2):
            to = half * cores + core
            send(chip_sum.at[half, pl.ds(12, 4)], from_north.at[chip], k_up, south, to)
            send(chip_sum.at[half, pl.ds(0, 4)], from_south.at[chip], k_down, north, to)
        send(chip_sum.at[1 - chip, pl.ds(HALO, 8)], from_chip, k_across, t, across)

    def reduced(chip_sum, from_chip, from_north, from_south, keys):
        key, k_across, k_up, k_down = keys
        arrived(from_chip, k_across)
        arrived(from_north, k_up)
        arrived(from_south, k_down)
        total = chip_sum[chip, pl.ds(HALO, 8)] + from_chip[...]
        edges = [from_north[0] + from_north[1], from_south[0] + from_south[1]]
        return total + jnp.concatenate(edges, axis=0)

    local_pass(x0, False)
    keys = (CR0, RZ0, RU0, RD0)
    reduce_in_chip(up, cr0, CR0)
    reduce_out(up, cr0, cs0, rz0, ru0, rd0, keys)
    state = (-STEP * scale * scale) * reduced(cs0, rz0, ru0, rd0, keys)
    state = jnp.concatenate(split2(state.reshape(64, LANES)), axis=0).astype(BF)

    def observe(which):
        for b in which:
            mixed = nn(state, onehot[b])
            mixed = mixed[:64] + mixed[64:]
            total = jnp.zeros((8, LANES), F32)
            for c in range(4):
                part = mixed[:, c * LANES : (c + 1) * LANES].reshape(8, 8, LANES)
                picked = jnp.sum(jnp.where(hits(b, c), part, 0.0), axis=0)
                total = total + feat[b, 20 + c : 21 + c, :] * picked
            y_own[b] = jnp.sum(feat[b, my_levels, :] * total, axis=0, keepdims=True)

    in_turn(observe)
    for d in range(1, groups):
        send(y_own, y_far.at[d - 1], YS, t, peer(d))
    arrived(y_far, YS)

    def misfit(b):
        y = y_own[b] + y_far[0, b] + y_far[1, b] + y_far[2, b]
        return feat[b, 25:26, :] * (y - feat[b, 24:25, :])

    acc[...] = jnp.zeros(acc.shape, F32)
    in_turn(lambda which: adjoint_obs(which, misfit))
    x1[j, pl.ds(HALO, 8)] = (-scale * STEP) * (STEP * x0[j, pl.ds(HALO, 8)] + summed())
    spread(x1, AC1, AZ1, AU1, AD1, FZ1, FU1, FD1)
    sent(cr0, CR0)
    local_pass(x1, True)

    sub = lax.broadcasted_iota(jnp.int32, (16, 8, LANES), 1)
    for lh in range(2):
        even, odd = up[lh * 2], up[lh * 2 + 1]
        vp[lh * 2] = jnp.where(sub < 4, even, pltpu.roll(odd, 4, 1))
        vp[lh * 2 + 1] = jnp.where(sub < 4, pltpu.roll(even, 4, 1), odd)

    def in_order(wide):
        hi, lo = split2(wide)
        return nn(hi.astype(BF), perm[1]) + nn(lo.astype(BF), perm[1])

    def written(m):
        return pltpu.make_async_copy(ready.at[m], control_ref.at[m], lsem.at[9 + m])

    def unmix(m):
        rows = pl.ds(m * 128, 128)
        wide = jnp.concatenate([flat[0, rows, :], flat[1, rows, :]], axis=1)
        ready[m] = in_order(wide).reshape(levels, 8, 256)
        written(m).start()

    keys = (CR1, RZ1, RU1, RD1)
    reduce_in_chip(vp, cr1, CR1)
    for m in range(members // 4):
        unmix(m)
    reduce_out(vp, cr1, cs1, rz1, ru1, rd1, keys)
    for m in range(members // 4, members):
        unmix(m)
    final = scale * reduced(cs1, rz1, ru1, rd1, keys)
    back = in_order(
        jnp.concatenate(
            [final.reshape(64, LANES), pltpu.roll(final, 4, 1).reshape(64, LANES)], axis=1
        )
    )
    for h in range(2):
        stage[h, 0:64, :] = back[:, h * LANES : (h + 1) * LANES]
        for level in range(4):
            incr_ref[level, :, h * LANES : (h + 1) * LANES] = stage[h, pl.ds(level, 8, stride=8), :]
    for m in range(members):
        written(m).wait()

    sent(in_buf.at[core, pl.ds(0, tiles - 1)], A2A)
    sent(kap_rows.at[0], KAP_U)
    sent(kap_rows.at[2], KAP_D)
    for part in range(len(PARTS)):
        part_sent(part)
    sent(in_buf.at[core], OBS)
    sent(y_far, YS)
    sent(cr1, CR1)
    for k in (AC0, AZ0, FZ0, RZ0, AC1, AZ1, FZ1, RZ1):
        sent(rz0, k)
    for k in (AU0, AD0, FU0, FD0, RU0, RD0, AU1, AD1, FU1, FD1, RU1, RD1):
        sent(ru0, k)


def on_device(tiles, groups, perturbations, classes, target, cells, interp, jac, innov, inverse):
    members, levels, rows, cols = perturbations.shape
    obs = target.shape[0]
    vm = pl.BlockSpec(memory_space=pltpu.VMEM)
    hbm = pl.BlockSpec(memory_space=pltpu.HBM)
    window = (groups, 16, 8, LANES)
    message = FEATURES * MOST // 2
    blocks = MOST * tiles // LANES
    reduction = [
        ((2, 16, 8, LANES), F32), ((2, 16, 8, LANES), F32), ((8, 8, LANES), F32),
        ((2, 4, 8, LANES), F32), ((2, 4, 8, LANES), F32),
    ]
    scratch = [
        (perturbations.shape, perturbations.dtype),
        (classes.shape, classes.dtype),
        ((1, obs), target.dtype),
        (cells.shape, cells.dtype),
        (interp.shape, interp.dtype),
        (jac.shape, jac.dtype),
        ((1, obs), innov.dtype),
        ((1, obs), inverse.dtype),
        ((2, 256, 256), BF),
        ((FEATURES, obs), F32),
        ((3, message, obs), BF),
        ((tiles, 1, message), F32),
        ((2, tiles, 1, message), F32),
        ((blocks, FEATURES, LANES), F32),
        ((blocks, LANES, 4 * LANES), BF),
        ((4, 128, 4 * LANES), BF),
        ((128, LANES), F32),
        ((16, 2, members * levels, LANES), F32),
        ((2, LANES, LANES), F32),
        ((3, 8, 256), F32),
        ((16, 2, 8, LANES), F32),
        ((8, 2, 8, LANES), F32),
        (window, F32), (window, F32), (window, F32), (window, F32),
        *reduction,
        *reduction,
        ((blocks, 1, LANES), F32),
        ((groups - 1, blocks, 1, LANES), F32),
        ((2, members * levels * rows, LANES), F32),
        ((members, levels, rows, cols), F32),
        ((2, 4, 2, members * levels // 2, LANES), F32),
    ]
    return pl.pallas_call(
        functools.partial(kernel, tiles, groups, members),
        out_shape=(
            jax.ShapeDtypeStruct((members, levels, rows, cols), F32),
            jax.ShapeDtypeStruct((levels // groups, rows, cols), F32),
        ),
        in_specs=[hbm] * 8,
        out_specs=(hbm, vm),
        scratch_shapes=[pltpu.VMEM(shape, dtype) for shape, dtype in scratch]
        + [
            pltpu.SemaphoreType.DMA((N_SEM,)),
            pltpu.SemaphoreType.DMA((N_SEM,)),
            pltpu.SemaphoreType.DMA((9 + members,)),
        ],
        compiler_params=pltpu.CompilerParams(
            collective_id=0, has_side_effects=True, vmem_limit_bytes=60 * 1024 * 1024
        ),
        name="assimilate",
    )(
        perturbations, classes, target.reshape(1, obs), cells, interp, jac,
        innov.reshape(1, obs), inverse.reshape(1, obs),
    )


def solution(mesh):
    in_specs = (
        P("mem", None, "tile", None),
        P("tile", None),
        P("tile", None),
        P(None, "tile"),
        P(None, "tile"),
        P(None, "tile"),
        P("tile"),
        P("tile"),
    )
    out_specs = (P("mem", None, "tile", None), P("mem", "tile", None))
    return jax.shard_map(
        functools.partial(on_device, mesh.shape["tile"], mesh.shape["mem"]),
        mesh=mesh, in_specs=in_specs, out_specs=out_specs, check_vma=False,
    )
```

profile of v0, /device:TPU:1, one launch (start us, length us, event | category | flops | bytes accessed | tf_op | source)
XLA Modules:
  0.0 79.1 jit_solution(18037991594486523427)
XLA Ops:
  0.6 75.5 %assimilate.1 = (f32[8,16,8,256]{3,2,1,0:T(8,128)}, f32[4,8,256]{2,1,0:T(8,128)}) custom-call(bf16[8,16,8,256]{3,2,1,0:T(8,128)(2,1)} %pert_hbm.1, s32[8,256]{1,0:T(8,128)} %classes_hbm.1, s32[1,1024]{1,0:T(1,128)} %bitcast.3, s32[4,1024]{1,0:T(4,128)} %cells_hbm.1, f32[4,1024]{1,0:T(4,128)} %interp_hbm.1, f32[16,1024]{1,0:T(8,128)} %jac_hbm.1, ...), custom_call_target="tpu_custom_call" | custom-call | tf_op jit(solution)/shard_map/assimilate/pallas_call | solution.py:596
  76.2 0.0 copy-start
  76.2 2.3 %copy.12 = f32[8,16,8,256]{3,2,1,0:T(8,128)} copy(f32[8,16,8,256]{3,2,1,0:T(8,128)} %get-tuple-element.4) | data formatting | bytes 2097152
  78.5 0.0 copy-done
  78.5 0.6 copy.13
Async XLA Ops:
  76.2 2.3 %copy-start = (f32[4,8,256]{2,1,0:T(8,128)S(1)}, f32[4,8,256]{2,1,0:T(8,128)}, u32[]{:S(2)}) copy-start(f32[4,8,256]{2,1,0:T(8,128)} %get-tuple-element.5) | copy-start | bytes 98308
where the time goes:
time: 79.2 us; the launch traced here: 79.1 us
  Pallas kernels  75.5 us (95%)
  local copies, waits for them, and re-layouts  2.89 us (4%)
    pallas_call x1, Pallas kernels, on_device(): pl.pallas_call(functools.partial(kernel, tiles, groups, members), out_sha...  75.5 us
    unnamed x4, local copies, waits for them, and re-layouts  2.89 us

commit v1 on v0

--- a/solution.py
+++ b/solution.py
@@ -193,20 +193,22 @@
         lo, hi = shares(part)[1]
         return relay.at[way, :, :, pl.ds(PARTS[part][0] // 2, hi - lo)]
 
-    def send_part(part):
+    def send_part(part, to_relay):
         one, two = shares(part)
         for way, (here, there, to, wraps, hop, onward) in enumerate(ways):
             key = key_of(way, part)
-
-            @pl.when(along_x == wraps)
-            def _():
-                send(edge(here, *two), waiting(way, part), key + 2, band(hop + tiles), j)
-
-            send(edge(here, *one), edge(there, *one), key, to, j)
-
-            @pl.when(along_x != wraps)
-            def _():
-                send(edge(here, *two), edge(there, *two), key + 1, to, j)
+            if to_relay:
+
+                @pl.when(along_x == wraps)
+                def _():
+                    send(edge(here, *two), waiting(way, part), key + 2, band(hop + tiles), j)
+
+            else:
+                send(edge(here, *one), edge(there, *one), key, to, j)
+
+                @pl.when(along_x != wraps)
+                def _():
+                    send(edge(here, *two), edge(there, *two), key + 1, to, j)
 
     def forward_part(part):
         two = shares(part)[1]
@@ -246,18 +248,20 @@
 
     send(kap_rows.at[1], kap_rows.at[0], KAP_U, south, j)
     send(kap_rows.at[1], kap_rows.at[2], KAP_D, north, j)
+    for part in range(len(PARTS)):
+        send_part(part, True)
     for part in range(early):
-        send_part(part)
+        send_part(part, False)
 
     def send_band(d, carry):
         send(out_buf.at[band(d)], in_buf.at[core, t], A2A, band(d), j)
         return carry
 
     lax.fori_loop(1, tiles, send_band, 0, unroll=9)
-    for part in range(early, len(PARTS)):
-        send_part(part)
-    for part in range(early):
+    for part in range(len(PARTS)):
         forward_part(part)
+        if part >= early:
+            send_part(part, False)
     own = pltpu.make_async_copy(out_buf.at[t], in_buf.at[core, t], lsem.at[0])
     own.start()
     arrived(kap_rows.at[0], KAP_U)
@@ -278,8 +282,6 @@
     own.wait()
     arrived(in_buf.at[core, pl.ds(0, tiles - 1)], A2A)
     send(in_buf.at[core], in_buf.at[core], OBS, t, sibling)
-    for part in range(early, len(PARTS)):
-        forward_part(part)
 
     blocks = MOST * tiles // LANES
     per_core = blocks // cores
@@ -293,7 +295,7 @@
                 at = source * per_core + g * 2 + b
                 feat[at] = both[b * FEATURES : (b + 1) * FEATURES, :]
 
-    along = 4
+    along = 12
 
     def in_turn(step, start=0, count=blocks):
         def several(i, carry):
@@ -311,11 +313,14 @@
         return rows == row.reshape(1, 1, LANES)
 
     def build(which):
+        spots = lax.broadcasted_iota(jnp.int32, (LANES, LANES), 0).astype(F32).astype(BF)
+        one, none = jnp.ones((), BF), jnp.zeros((), BF)
         for b in which:
+            low = (feat[b, 16:24, :].astype(jnp.int32) & 255) >> 1
+            low = low.astype(F32).astype(BF)
             for c in range(4):
-                low = (feat[b, 16 + c : 17 + c, :].astype(jnp.int32) & 255) >> 1
-                spot = lax.broadcasted_iota(jnp.int32, (LANES, LANES), 0) == low
-                onehot[b, :, c * LANES : (c + 1) * LANES] = jnp.where(spot, 1.0, 0.0).astype(BF)
+                spot = spots == low[c : c + 1, :]
+                onehot[b, :, c * LANES : (c + 1) * LANES] = jnp.where(spot, one, none)
 
     def adjoint_obs(which, residual):
         for n, b in enumerate(which):
@@ -577,7 +582,7 @@
         ((2, tiles, 1, message), F32),
         ((blocks, FEATURES, LANES), F32),
         ((blocks, LANES, 4 * LANES), BF),
-        ((4, 128, 4 * LANES), BF),
+        ((12, 128, 4 * LANES), BF),
         ((128, LANES), F32),
         ((16, 2, members * levels, LANES), F32),
         ((2, LANES, LANES), F32),

time: 79.2 us -> 77.7 us (0.981)
  Pallas kernels: 75.5 us -> 74 us
    pallas_call x1, Pallas kernels: 75.5 us -> 74 us  [on_device(): pl.pallas_call(functools.partial(kernel, tiles, groups, members), out_sha...]
where the time goes in v1:
time: 77.7 us; the launch traced here: 77.6 us
  Pallas kernels  74 us (95%)
  local copies, waits for them, and re-layouts  2.89 us (4%)
    pallas_call x1, Pallas kernels, on_device(): pl.pallas_call(functools.partial(kernel, tiles, groups, members), out_sha...  74 us
    unnamed x4, local copies, waits for them, and re-layouts  2.89 us

profile of v1, /device:TPU:1, one launch (start us, length us, event | category | flops | bytes accessed | tf_op | source)
XLA Modules:
  0.0 77.6 jit_solution(13034888227163184098)
XLA Ops:
  0.6 74.0 %assimilate.1 = (f32[8,16,8,256]{3,2,1,0:T(8,128)}, f32[4,8,256]{2,1,0:T(8,128)}) custom-call(bf16[8,16,8,256]{3,2,1,0:T(8,128)(2,1)} %pert_hbm.1, s32[8,256]{1,0:T(8,128)} %classes_hbm.1, s32[1,1024]{1,0:T(1,128)} %bitcast.3, s32[4,1024]{1,0:T(4,128)} %cells_hbm.1, f32[4,1024]{1,0:T(4,128)} %interp_hbm.1, f32[16,1024]{1,0:T(8,128)} %jac_hbm.1, ...), custom_call_target="tpu_custom_call" | custom-call | tf_op jit(solution)/shard_map/assimilate/pallas_call | solution.py:601
  74.7 0.0 copy-start
  74.7 2.3 %copy.12 = f32[8,16,8,256]{3,2,1,0:T(8,128)} copy(f32[8,16,8,256]{3,2,1,0:T(8,128)} %get-tuple-element.4) | data formatting | bytes 2097152
  77.0 0.0 copy-done
  77.0 0.6 copy.13
Async XLA Ops:
  74.7 2.3 %copy-start = (f32[4,8,256]{2,1,0:T(8,128)S(1)}, f32[4,8,256]{2,1,0:T(8,128)}, u32[]{:S(2)}) copy-start(f32[4,8,256]{2,1,0:T(8,128)} %get-tuple-element.5) | copy-start | bytes 98308

commit v2 on v1

--- a/solution.py
+++ b/solution.py
@@ -83,9 +83,9 @@
     fetches = [
         pltpu.make_async_copy(source, into, lsem.at[1 + k])
         for k, (source, into) in enumerate((
+            (pert_hbm, pert_ref), (classes_hbm, classes_ref),
             (target_hbm, target_ref), (cells_hbm, cells_ref), (interp_hbm, interp_ref),
             (jac_hbm, jac_ref), (innov_hbm, innov_ref), (inv_hbm, inv_ref),
-            (pert_hbm, pert_ref), (classes_hbm, classes_ref),
         ))
     ]
     for fetch in fetches:
@@ -113,7 +113,113 @@
     perm[0] = jnp.where(col_id == (row_id & 1) * 128 + (row_id >> 1), 1.0, 0.0).astype(BF)
     perm[1] = jnp.where(row_id == (col_id & 1) * 128 + (col_id >> 1), 1.0, 0.0).astype(BF)
 
-    for fetch in fetches[:6]:
+    for fetch in fetches[:2]:
+        fetch.wait()
+
+    def arrange(m, carry):
+        block = pert_ref[m].astype(F32).reshape(levels * 8, 256).astype(BF)
+        moved = nn(block, perm[0])
+        stage[0] = moved[:, :LANES]
+        stage[1] = moved[:, LANES:]
+        for r in range(8):
+            for lh in range(2):
+                at = pl.ds(pl.multiple_of(m * levels + lh * 8, 8), 8)
+                for h in range(2):
+                    pert[HALO + r, h, at, :] = stage[h, pl.ds(lh * 64 + r, 8, stride=8), :]
+        return carry
+
+    lax.fori_loop(0, members, arrange, 0)
+
+    classes = nn(classes_ref[...].astype(F32).astype(BF), perm[0])
+    kappa = jnp.zeros(classes.shape, F32)
+    for position, coefficient in enumerate(DIFFUSIVITIES):
+        kappa = kappa + jnp.where(classes == float(position), coefficient, 0.0)
+    kap_rows[1] = kappa
+
+    pl.semaphore_wait(barrier, tiles - 1 + groups - 1 + 2)
+
+    along_x = lax.rem(t, 4)
+    ways = (
+        (8, 0, south, 3, -3, 4),
+        (4, 12, north, 0, 3, -4),
+    )
+
+    def edge(first_row, lo, hi):
+        return pert.at[pl.ds(first_row, 4), :, pl.ds(lo, hi - lo)]
+
+    def shares(part):
+        lo, hi = PARTS[part]
+        middle = (lo + hi) // 2
+        return (lo, middle), (middle, hi)
+
+    def key_of(way, part):
+        return PERT + (way * len(PARTS) + part) * 4
+
+    def waiting(way, part):
+        lo, hi = shares(part)[1]
+        return relay.at[way, :, :, pl.ds(PARTS[part][0] // 2, hi - lo)]
+
+    def send_part(part, to_relay):
+        one, two = shares(part)
+        for way, (here, there, to, wraps, hop, onward) in enumerate(ways):
+            key = key_of(way, part)
+            if to_relay:
+
+                @pl.when(along_x == wraps)
+                def _():
+                    send(edge(here, *two), waiting(way, part), key + 2, band(hop + tiles), j)
+
+            else:
+                send(edge(here, *one), edge(there, *one), key, to, j)
+
+                @pl.when(along_x != wraps)
+                def _():
+                    send(edge(here, *two), edge(there, *two), key + 1, to, j)
+
+    def forward_part(part):
+        two = shares(part)[1]
+        for way, (here, there, to, wraps, hop, onward) in enumerate(ways):
+            key = key_of(way, part)
+
+            @pl.when(along_x == 3 - wraps)
+            def _():
+                arrived(waiting(way, part), key + 2)
+                send(
+                    waiting(way, part), edge(there, *two), key + 1, band(onward + tiles), j, key + 3
+                )
+
+    def part_arrived(part):
+        one, two = shares(part)
+        for way, (here, there, to, wraps, hop, onward) in enumerate(ways):
+            arrived(edge(there, *one), key_of(way, part))
+            arrived(edge(there, *two), key_of(way, part) + 1)
+
+    def part_sent(part):
+        one, two = shares(part)
+        for way, (here, there, to, wraps, hop, onward) in enumerate(ways):
+            key = key_of(way, part)
+            sent(edge(here, *one), key)
+
+            @pl.when(along_x == wraps)
+            def _():
+                sent(edge(here, *two), key + 2)
+
+            @pl.when(along_x != wraps)
+            def _():
+                sent(edge(here, *two), key + 1)
+
+            @pl.when(along_x == 3 - wraps)
+            def _():
+                sent(waiting(way, part), key + 3)
+
+    send(kap_rows.at[1], kap_rows.at[0], KAP_U, south, j)
+    send(kap_rows.at[1], kap_rows.at[2], KAP_D, north, j)
+    for part in range(len(PARTS)):
+        send_part(part, True)
+    for part in range(early):
+        send_part(part, False)
+
+    for fetch in fetches[2:]:
         fetch.wait()
 
     target = target_ref[...]
@@ -146,112 +252,6 @@
             val[k, q * FEATURES : (q + 1) * FEATURES, :] = jnp.where(mine, piece, 0.0).astype(BF)
     packed = nt(member_bf, val[0]) + nt(member_bf, val[1]) + nt(member_bf, val[2])
     out_buf[:, 0, :] = packed
-
-    for fetch in fetches[6:]:
-        fetch.wait()
-
-    def arrange(m, carry):
-        block = pert_ref[m].astype(F32).reshape(levels * 8, 256).astype(BF)
-        moved = nn(block, perm[0])
-        stage[0] = moved[:, :LANES]
-        stage[1] = moved[:, LANES:]
-        for r in range(8):
-            for lh in range(2):
-                at = pl.ds(pl.multiple_of(m * levels + lh * 8, 8), 8)
-                for h in range(2):
-                    pert[HALO + r, h, at, :] = stage[h, pl.ds(lh * 64 + r, 8, stride=8), :]
-        return carry
-
-    lax.fori_loop(0, members, arrange, 0)
-
-    classes = nn(classes_ref[...].astype(F32).astype(BF), perm[0])
-    kappa = jnp.zeros(classes.shape, F32)
-    for position, coefficient in enumerate(DIFFUSIVITIES):
-        kappa = kappa + jnp.where(classes == float(position), coefficient, 0.0)
-    kap_rows[1] = kappa
-
-    pl.semaphore_wait(barrier, tiles - 1 + groups - 1 + 2)
-
-    along_x = lax.rem(t, 4)
-    ways = (
-        (8, 0, south, 3, -3, 4),
-        (4, 12, north, 0, 3, -4),
-    )
-
-    def edge(first_row, lo, hi):
-        return pert.at[pl.ds(first_row, 4), :, pl.ds(lo, hi - lo)]
-
-    def shares(part):
-        lo, hi = PARTS[part]
-        middle = (lo + hi) // 2
-        return (lo, middle), (middle, hi)
-
-    def key_of(way, part):
-        return PERT + (way * len(PARTS) + part) * 4
-
-    def waiting(way, part):
-        lo, hi = shares(part)[1]
-        return relay.at[way, :, :, pl.ds(PARTS[part][0] // 2, hi - lo)]
-
-    def send_part(part, to_relay):
-        one, two = shares(part)
-        for way, (here, there, to, wraps, hop, onward) in enumerate(ways):
-            key = key_of(way, part)
-            if to_relay:
-
-                @pl.when(along_x == wraps)
-                def _():
-                    send(edge(here, *two), waiting(way, part), key + 2, band(hop + tiles), j)
-
-            else:
-                send(edge(here, *one), edge(there, *one), key, to, j)
-
-                @pl.when(along_x != wraps)
-                def _():
-                    send(edge(here, *two), edge(there, *two), key + 1, to, j)
-
-    def forward_part(part):
-        two = shares(part)[1]
-        for way, (here, there, to, wraps, hop, onward) in enumerate(ways):
-            key = key_of(way, part)
-
-            @pl.when(along_x == 3 - wraps)
-            def _():
-                arrived(waiting(way, part), key + 2)
-                send(
-                    waiting(way, part), edge(there, *two), key + 1, band(onward + tiles), j, key + 3
-                )
-
-    def part_arrived(part):
-        one, two = shares(part)
-        for way, (here, there, to, wraps, hop, onward) in enumerate(ways):
-            arrived(edge(there, *one), key_of(way, part))
-            arrived(edge(there, *two), key_of(way, part) + 1)
-
-    def part_sent(part):
-        one, two = shares(part)
-        for way, (here, there, to, wraps, hop, onward) in enumerate(ways):
-            key = key_of(way, part)
-            sent(edge(here, *one), key)
-
-            @pl.when(along_x == wraps)
-            def _():
-                sent(edge(here, *two), key + 2)
-
-            @pl.when(along_x != wraps)
-            def _():
-                sent(edge(here, *two), key + 1)
-
-            @pl.when(along_x == 3 - wraps)
-            def _():
-                sent(waiting(way, part), key + 3)
-
-    send(kap_rows.at[1], kap_rows.at[0], KAP_U, south, j)
-    send(kap_rows.at[1], kap_rows.at[2], KAP_D, north, j)
-    for part in range(len(PARTS)):
-        send_part(part, True)
-    for part in range(early):
-        send_part(part, False)
 
     def send_band(d, carry):
         send(out_buf.at[band(d)], in_buf.at[core, t], A2A, band(d), j)
@@ -552,6 +552,21 @@
         sent(rz0, k)
     for k in (AU0, AD0, FU0, FD0, RU0, RD0, AU1, AD1, FU1, FD1, RU1, RD1):
         sent(ru0, k)
+
+
+def write_out(control_ref, incr_ref, control_out, incr_out, control_held, incr_held, sems):
+    count = control_ref.shape[0]
+    ways = [(control_ref.at[m], control_held.at[m], control_out.at[m]) for m in range(count)]
+    ways.append((incr_ref, incr_held, incr_out))
+    reads = [pltpu.make_async_copy(a, b, sems.at[0, n]) for n, (a, b, c) in enumerate(ways)]
+    writes = [pltpu.make_async_copy(b, c, sems.at[1, n]) for n, (a, b, c) in enumerate(ways)]
+    for read in reads:
+        read.start()
+    for read, write in zip(reads, writes):
+        read.wait()
+        write.start()
+    for write in writes:
+        write.wait()
 
 
 def on_device(tiles, groups, perturbations, classes, target, cells, interp, jac, innov, inverse):
@@ -598,7 +613,7 @@
         ((members, levels, rows, cols), F32),
         ((2, 4, 2, members * levels // 2, LANES), F32),
     ]
-    return pl.pallas_call(
+    control, increment = pl.pallas_call(
         functools.partial(kernel, tiles, groups, members),
         out_shape=(
             jax.ShapeDtypeStruct((members, levels, rows, cols), F32),
@@ -620,6 +635,21 @@
         perturbations, classes, target.reshape(1, obs), cells, interp, jac,
         innov.reshape(1, obs), inverse.reshape(1, obs),
     )
+    return pl.pallas_call(
+        write_out,
+        out_shape=(
+            jax.ShapeDtypeStruct(control.shape, F32), jax.ShapeDtypeStruct(increment.shape, F32)
+        ),
+        in_specs=[hbm, hbm],
+        out_specs=(hbm, hbm),
+        scratch_shapes=[
+            pltpu.VMEM(control.shape, F32),
+            pltpu.VMEM(increment.shape, F32),
+            pltpu.SemaphoreType.DMA((2, members + 1)),
+        ],
+        compiler_params=pltpu.CompilerParams(vmem_limit_bytes=60 * 1024 * 1024),
+        name="write_out",
+    )(control, increment)
 
 
 def solution(mesh):

time: 77.7 us -> 76.6 us (0.986)
  local copies, waits for them, and re-layouts: 2.89 us -> 0 us
  Pallas kernels: 74 us -> 75.6 us
    unnamed x4 -> x0, local copies, waits for them, and re-layouts: 2.89 us -> none
    pallas_call x0 -> x1, Pallas kernels: none -> 2.11 us  [on_device(): pl.pallas_call(write_out, out_shape=(jax.ShapeDtypeStruct(control.shape,...]
where the time goes in v2:
time: 76.6 us; the launch traced here: 76.3 us
  Pallas kernels  75.6 us (99%)
    pallas_call x1, Pallas kernels, on_device(): pl.pallas_call(functools.partial(kernel, tiles, groups, members), out_sha...  73.5 us
    pallas_call x1, Pallas kernels, on_device(): pl.pallas_call(write_out, out_shape=(jax.ShapeDtypeStruct(control.shape,...  2.11 us

profile of v2, /device:TPU:1, one launch (start us, length us, event | category | flops | bytes accessed | tf_op | source)
XLA Modules:
  0.0 76.3 jit_solution(5219407343570352141)
XLA Ops:
  0.6 73.5 %assimilate.1 = (f32[8,16,8,256]{3,2,1,0:T(8,128)}, f32[4,8,256]{2,1,0:T(8,128)}) custom-call(bf16[8,16,8,256]{3,2,1,0:T(8,128)(2,1)} %pert_hbm.1, s32[8,256]{1,0:T(8,128)} %classes_hbm.1, s32[1,1024]{1,0:T(1,128)} %bitcast.3, s32[4,1024]{1,0:T(4,128)} %cells_hbm.1, f32[4,1024]{1,0:T(4,128)} %interp_hbm.1, f32[16,1024]{1,0:T(8,128)} %jac_hbm.1, ...), custom_call_target="tpu_custom_call" | custom-call | tf_op jit(solution)/shard_map/assimilate/pallas_call | solution.py:616
  74.2 2.1 %write_out.1 = (f32[8,16,8,256]{3,2,1,0:T(8,128)}, f32[4,8,256]{2,1,0:T(8,128)}) custom-call(f32[8,16,8,256]{3,2,1,0:T(8,128)} %get-tuple-element.4.control_ref, f32[4,8,256]{2,1,0:T(8,128)} %get-tuple-element.5.incr_ref), custom_call_target="tpu_custom_call" | custom-call | tf_op jit(solution)/shard_map/write_out/pallas_call | solution.py:638

commit v3 on v2

--- a/solution.py
+++ b/solution.py
@@ -116,19 +116,24 @@
     for fetch in fetches[:2]:
         fetch.wait()
 
-    def arrange(m, carry):
-        block = pert_ref[m].astype(F32).reshape(levels * 8, 256).astype(BF)
-        moved = nn(block, perm[0])
-        stage[0] = moved[:, :LANES]
-        stage[1] = moved[:, LANES:]
-        for r in range(8):
-            for lh in range(2):
-                at = pl.ds(pl.multiple_of(m * levels + lh * 8, 8), 8)
-                for h in range(2):
-                    pert[HALO + r, h, at, :] = stage[h, pl.ds(lh * 64 + r, 8, stride=8), :]
+    def arrange(i, carry):
+        some = [i * 4 + n for n in range(4)]
+        for m in some:
+            block = pert_ref[m].astype(F32).reshape(levels * 8, 256).astype(BF)
+            moved = nn(block, perm[0])
+            rows = pl.ds(pl.multiple_of(m * 128, 128), 128)
+            for h in range(2):
+                flat[h, rows, :] = moved[:, h * LANES : (h + 1) * LANES]
+        for m in some:
+            for r in range(8):
+                for lh in range(2):
+                    at = pl.ds(pl.multiple_of(m * levels + lh * 8, 8), 8)
+                    for h in range(2):
+                        rows = pl.ds(m * 128 + lh * 64 + r, 8, stride=8)
+                        pert[HALO + r, h, at, :] = flat[h, rows, :]
         return carry
 
-    lax.fori_loop(0, members, arrange, 0)
+    lax.fori_loop(0, members // 4, arrange, 0)
 
     classes = nn(classes_ref[...].astype(F32).astype(BF), perm[0])
     kappa = jnp.zeros(classes.shape, F32)
@@ -242,15 +247,14 @@
         [innov_ref[...], inv_ref[...], jnp.zeros((6, obs), F32)], axis=0
     )
     whole = pay[...]
-    high = whole.astype(BF).astype(F32)
-    rest = whole - high
-    middle = rest.astype(BF).astype(F32)
-    low = rest - middle
+    pieces = [piece.astype(BF) for piece in split2(whole)]
+    rank = rank.astype(F32).astype(BF)
+    nothing = jnp.zeros((), BF)
     for q in range(slots):
-        mine = rank == q
-        for k, piece in enumerate((high, middle, low)):
-            val[k, q * FEATURES : (q + 1) * FEATURES, :] = jnp.where(mine, piece, 0.0).astype(BF)
-    packed = nt(member_bf, val[0]) + nt(member_bf, val[1]) + nt(member_bf, val[2])
+        mine = rank == jnp.full((), q, BF)
+        for k, piece in enumerate(pieces):
+            val[k, q * FEATURES : (q + 1) * FEATURES, :] = jnp.where(mine, piece, nothing)
+    packed = nt(member_bf, val[0]) + nt(member_bf, val[1])
     out_buf[:, 0, :] = packed
 
     def send_band(d, carry):
@@ -592,7 +596,7 @@
         ((1, obs), inverse.dtype),
         ((2, 256, 256), BF),
         ((FEATURES, obs), F32),
-        ((3, message, obs), BF),
+        ((2, message, obs), BF),
         ((tiles, 1, message), F32),
         ((2, tiles, 1, message), F32),
         ((blocks, FEATURES, LANES), F32),

time: 76.6 us -> 76.7 us (level)
  no operation moved by 1% of the time
where the time goes in v3:
time: 76.7 us; the launch traced here: 76.5 us
  Pallas kernels  75.9 us (99%)
    pallas_call x1, Pallas kernels, on_device(): pl.pallas_call(functools.partial(kernel, tiles, groups, members), out_sha...  73.8 us
    pallas_call x1, Pallas kernels, on_device(): pl.pallas_call(write_out, out_shape=(jax.ShapeDtypeStruct(control.shape,...  2.11 us

profile of v3, /device:TPU:1, one launch (start us, length us, event | category | flops | bytes accessed | tf_op | source)
XLA Modules:
  0.0 76.5 jit_solution(16576881959061574998)
XLA Ops:
  0.6 73.8 %assimilate.1 = (f32[8,16,8,256]{3,2,1,0:T(8,128)}, f32[4,8,256]{2,1,0:T(8,128)}) custom-call(bf16[8,16,8,256]{3,2,1,0:T(8,128)(2,1)} %pert_hbm.1, s32[8,256]{1,0:T(8,128)} %classes_hbm.1, s32[1,1024]{1,0:T(1,128)} %bitcast.3, s32[4,1024]{1,0:T(4,128)} %cells_hbm.1, f32[4,1024]{1,0:T(4,128)} %interp_hbm.1, f32[16,1024]{1,0:T(8,128)} %jac_hbm.1, ...), custom_call_target="tpu_custom_call" | custom-call | tf_op jit(solution)/shard_map/assimilate/pallas_call | solution.py:620
  74.4 2.1 %write_out.1 = (f32[8,16,8,256]{3,2,1,0:T(8,128)}, f32[4,8,256]{2,1,0:T(8,128)}) custom-call(f32[8,16,8,256]{3,2,1,0:T(8,128)} %get-tuple-element.4.control_ref, f32[4,8,256]{2,1,0:T(8,128)} %get-tuple-element.5.incr_ref), custom_call_target="tpu_custom_call" | custom-call | tf_op jit(solution)/shard_map/write_out/pallas_call | solution.py:642

commit v4 on v2

--- a/solution.py
+++ b/solution.py
@@ -21,7 +21,7 @@
 (A2A, KAP_U, KAP_D, OBS, AC0, AZ0, AU0, AD0, FZ0, FU0, FD0, CR0, RZ0, RU0, RD0, YS,
  AC1, AZ1, AU1, AD1, FZ1, FU1, FD1, CR1, RZ1, RU1, RD1, PERT) = range(28)
 PARTS = ((0, 32), (32, 64), (64, 128))
-EARLY = 1
+EARLY = 2
 N_SEM = PERT + 8 * len(PARTS)
 
 

time: 76.6 us -> 77.4 us (1.010)
  Pallas kernels: 75.6 us -> 76.5 us
    pallas_call x1, Pallas kernels: 73.5 us -> 74.4 us  [on_device(): pl.pallas_call(functools.partial(kernel, tiles, groups, members), out_sha...]
where the time goes in v4:
time: 77.4 us; the launch traced here: 77.1 us
  Pallas kernels  76.5 us (99%)
    pallas_call x1, Pallas kernels, on_device(): pl.pallas_call(functools.partial(kernel, tiles, groups, members), out_sha...  74.4 us
    pallas_call x1, Pallas kernels, on_device(): pl.pallas_call(write_out, out_shape=(jax.ShapeDtypeStruct(control.shape,...  2.11 us

profile of v4, /device:TPU:1, one launch (start us, length us, event | category | flops | bytes accessed | tf_op | source)
XLA Modules:
  0.0 77.1 jit_solution(13400269841668684719)
XLA Ops:
  0.6 74.4 %assimilate.1 = (f32[8,16,8,256]{3,2,1,0:T(8,128)}, f32[4,8,256]{2,1,0:T(8,128)}) custom-call(bf16[8,16,8,256]{3,2,1,0:T(8,128)(2,1)} %pert_hbm.1, s32[8,256]{1,0:T(8,128)} %classes_hbm.1, s32[1,1024]{1,0:T(1,128)} %bitcast.3, s32[4,1024]{1,0:T(4,128)} %cells_hbm.1, f32[4,1024]{1,0:T(4,128)} %interp_hbm.1, f32[16,1024]{1,0:T(8,128)} %jac_hbm.1, ...), custom_call_target="tpu_custom_call" | custom-call | tf_op jit(solution)/shard_map/assimilate/pallas_call | solution.py:616
  75.0 2.1 %write_out.1 = (f32[8,16,8,256]{3,2,1,0:T(8,128)}, f32[4,8,256]{2,1,0:T(8,128)}) custom-call(f32[8,16,8,256]{3,2,1,0:T(8,128)} %get-tuple-element.4.control_ref, f32[4,8,256]{2,1,0:T(8,128)} %get-tuple-element.5.incr_ref), custom_call_target="tpu_custom_call" | custom-call | tf_op jit(solution)/shard_map/write_out/pallas_call | solution.py:638
